TPU v7x, 512 devices: a whole 4x8x8 slice. The times are simulated.
512 devices in a mesh: dp: 32 (over x, z), seq: 16 (over y, core).
Axes of the slice: x: 4, y: 8, z: 8, core: 2. Of those that a mesh axis runs over, the one named last changes fastest.
Arguments:
- projected: bfloat16 [32, 2048, 3, 1536], P('dp', 'seq'), may hold values from -6 to 6
- cotangent: bfloat16 [32, 2048, 1152], P('dp', 'seq'), may hold values from -6 to 6
- out_weight: bfloat16 [1536, 1152], P('seq'), may hold values from -0.15625 to 0.15625
- norm_gain: float32 [1536], replicated, may hold values from 0.1 to 1.9
- conv_taps: float32 [9, 1536], replicated, may hold values from -2.5 to 2.5
- feature_seeds: int32 [48], replicated, may hold values from 0 to 1073741823
- packing: int32 [32, 5, 2048], P('dp', None, 'seq'), may hold values from 0 to 68, as said below
Outputs:
- block_out: bfloat16 [32, 2048, 1152], P('dp', 'seq')
- grad_projected: bfloat16 [32, 2048, 3, 1536], P('dp', 'seq')
- grad_out_weight: float32 [1536, 1152], P('seq')
- grad_norm_gain: float32 [1536], replicated
- grad_conv_taps: float32 [9, 1536], replicated
Inputs may be any that keep to these rules, and one draw needn't show every extreme that they name: `packing`: in each pack, images 0 to 2 follow one another, each contiguous and row-major; rows 1 and 2 give a token's row and column in its image, rows 3 and 4 the image's width and height. Widths are multiples of 16 up to 64; image 1 of every pack is 64 wide and directly precedes the last image; the last image of every pack is 16 wide and holds the pack's last 1088 tokens; heights are at least 2; every pack holds 3 images and no padding.
All inputs are finite; a program needn't handle non-finite values.
Results may differ from a plain program's by a relative error of at most 0.012.
Values may be sent and summed in bfloat16 or wider, within the bound.
No kernel may reach another device: no remote copies, remote signals or barrier semaphores. Data moves between devices by JAX's collectives and lax.ppermute only.
A program may use at most 128 MiB of HBM per device.

v0:
```python
import math
import jax
import jax.numpy as jnp
from jax import lax
from jax.sharding import PartitionSpec as P

HEAD = 32
FEAT = 256
IMGS = 3
WMAX = 64
feature_floor = 0.1
epsilon = 1e-06
highest = lax.Precision.HIGHEST


def with_halo(shard, sides, width):
    for axis, dim in sides:
        devices, length = (lax.axis_size(axis), shard.shape[dim])
        up = [(i, (i + 1) % devices) for i in range(devices - 1)]
        down = [(j, i) for i, j in up]
        last = lax.slice_in_dim(shard, length - width, length, axis=dim)
        initial = lax.slice_in_dim(shard, 0, width, axis=dim)
        before = lax.ppermute(last, axis, up)
        after = lax.ppermute(initial, axis, down)
        shard = jnp.concatenate([before, shard, after], axis=dim)
    return shard


def feature_matrix(seed_list):
    counter = jnp.arange(HEAD * FEAT, dtype=jnp.int32).reshape(1, HEAD, FEAT)
    hashed = seed_list[:, None, None] * -1640531535 + counter
    hashed = hashed ^ hashed >> 16 & 65535
    hashed = hashed * -2048144789
    hashed = hashed ^ hashed >> 13 & 524287
    hashed = hashed * -1028477387
    hashed = hashed ^ hashed >> 16 & 65535
    top_bits = hashed >> 8 & 16777215
    uniform = top_bits.astype(jnp.float32) * (1.0 / 16777216.0)
    return (1.7320508 * (2.0 * uniform - 1.0)).astype(jnp.bfloat16)


def neighbour(padded, margin, packing_rows, tap_index, direction):
    row_count = packing_rows.shape[1]
    step_row = tap_index // 3 - 1
    step_col = tap_index % 3 - 1
    position = jnp.arange(row_count, dtype=jnp.int32)
    row_width = packing_rows[3]
    new_row = packing_rows[1] + direction * step_row
    new_col = packing_rows[2] + direction * step_col
    inside = (new_row >= 0) & (new_row < packing_rows[4]) & (new_col >= 0) & (new_col < row_width)
    source = position + margin + direction * (step_row * row_width + step_col)
    return jnp.where(inside[:, None], jnp.take(padded, source, axis=0), jnp.zeros((), padded.dtype))


def depthwise(padded, margin, packing_rows, tap_table, direction):
    running = jnp.zeros((packing_rows.shape[1], padded.shape[1]), jnp.float32)
    for tap_index in range(9):
        running = running + tap_table[tap_index][None, :] * neighbour(
            padded, margin, packing_rows, tap_index, direction
        ).astype(jnp.float32)
    return running


def tap_grads(grad_conv, padded, margin, packing_rows):
    grad_float = grad_conv.astype(jnp.float32)
    return jnp.stack(
        [
            jnp.sum(
                grad_float
                * neighbour(padded, margin, packing_rows, tap_index, 1).astype(jnp.float32),
                axis=0,
            )
            for tap_index in range(9)
        ]
    )


def heads_last(rows_matrix, head_count):
    return rows_matrix.reshape(rows_matrix.shape[0], head_count, HEAD).transpose(1, 2, 0)


def rows_first(head_matrix):
    return head_matrix.transpose(2, 0, 1).reshape(
        head_matrix.shape[2], head_matrix.shape[0] * head_matrix.shape[1]
    )


def local(projected, cotangent, out_weight, norm_gain, conv_taps, feature_seeds, packing):
    groups = lax.axis_size("seq")
    member = lax.axis_index("seq")
    pack_count = lax.axis_size("dp")
    tokens_in = projected[0]
    grad_in = cotangent[0]
    rows_local = packing[0]
    tok_rows = tokens_in.shape[0]
    width_all = tokens_in.shape[2]
    local_width = width_all // groups
    head_count = local_width // HEAD
    all_rows = tok_rows * groups
    margin = WMAX + 1
    feature_scale = 1.0 / math.sqrt(HEAD)
    rows_all = lax.all_gather(rows_local, "seq", axis=1, tiled=True)
    padded_values = with_halo(tokens_in[:, 2], (("seq", 0),), margin)
    conv_tokens = depthwise(padded_values, margin, rows_local, conv_taps, 1).astype(jnp.bfloat16)
    outgoing = jnp.stack([tokens_in[:, 0], tokens_in[:, 1], conv_tokens], axis=1)
    arrived = lax.all_to_all(
        outgoing.reshape(tok_rows, 3, groups, local_width),
        "seq",
        split_axis=2,
        concat_axis=0,
        tiled=True,
    )
    arrived = arrived.reshape(all_rows, 3, local_width)
    conv_heads = arrived[:, 2]
    omegas = feature_matrix(
        lax.dynamic_slice_in_dim(feature_seeds, member * head_count, head_count, 0)
    )
    queries = heads_last(arrived[:, 0], head_count)
    keys_in = heads_last(arrived[:, 1], head_count)
    values_c = heads_last(conv_heads, head_count)
    onehot_float = (jnp.arange(IMGS, dtype=jnp.int32)[:, None] == rows_all[0][None, :]).astype(
        jnp.float32
    )
    onehot_half = onehot_float.astype(jnp.bfloat16)
    pre_query = (
        jnp.einsum("het,hef->hft", queries, omegas, preferred_element_type=jnp.float32)
        * feature_scale
    )
    pre_key = (
        jnp.einsum("het,hef->hft", keys_in, omegas, preferred_element_type=jnp.float32)
        * feature_scale
    )
    feat_query = (jax.nn.relu(pre_query) + feature_floor).astype(jnp.bfloat16)
    feat_key = (jax.nn.relu(pre_key) + feature_floor).astype(jnp.bfloat16)
    masked_values = onehot_half[None, :, None, :] * values_c[:, None]
    states = jnp.einsum(
        "hft,hiet->hife", feat_key, masked_values, preferred_element_type=jnp.float32
    ).astype(jnp.bfloat16)
    totals = jnp.einsum(
        "hft,it->hif", feat_key, onehot_half, preferred_element_type=jnp.float32
    ).astype(jnp.bfloat16)
    numerator = jnp.sum(
        jnp.einsum("hft,hife->hiet", feat_query, states, preferred_element_type=jnp.float32)
        * onehot_float[None, :, None, :],
        axis=1,
    )
    denominator = jnp.sum(
        jnp.einsum("hft,hif->hit", feat_query, totals, preferred_element_type=jnp.float32)
        * onehot_float[None],
        axis=1,
    )
    attention_heads = rows_first(
        (numerator / denominator[:, None, :]).astype(jnp.bfloat16)
    ).reshape(all_rows, 1, local_width)
    attention = lax.all_to_all(
        attention_heads, "seq", split_axis=0, concat_axis=1, tiled=True
    ).reshape(tok_rows, width_all)
    attn_float = attention.astype(jnp.float32)
    inv_rms = lax.rsqrt(jnp.mean(attn_float * attn_float, axis=1) + epsilon)
    normed = (attn_float * norm_gain[None, :] * inv_rms[:, None]).astype(jnp.bfloat16)
    weight_all = lax.all_gather(out_weight, "seq", axis=0, tiled=True)
    block_sum = jnp.dot(normed, weight_all, preferred_element_type=jnp.float32)
    grad_normed = jnp.einsum("td,ad->ta", grad_in, weight_all, preferred_element_type=jnp.float32)
    pack_gain = jnp.sum(grad_normed * attn_float * inv_rms[:, None], axis=0)
    inner_sum = jnp.sum(norm_gain[None, :] * grad_normed * attn_float, axis=1)
    grad_attention = (
        inv_rms[:, None] * norm_gain[None, :] * grad_normed
        - attn_float * (inv_rms**3 * inner_sum / width_all)[:, None]
    ).astype(jnp.bfloat16)
    grad_arrived, normed_heads = (
        lax.all_to_all(
            grad_attention.reshape(tok_rows, groups, local_width),
            "seq",
            split_axis=1,
            concat_axis=0,
            tiled=True,
        ),
        lax.all_to_all(
            normed.reshape(tok_rows, groups, local_width),
            "seq",
            split_axis=1,
            concat_axis=0,
            tiled=True,
        ),
    )
    normed_rows = normed_heads.reshape(all_rows, local_width)
    weight_local = jnp.einsum(
        "tc,td->cd",
        normed_rows,
        lax.all_gather(grad_in, "seq", axis=0, tiled=True),
        preferred_element_type=jnp.float32,
    )
    weight_sum = lax.psum(weight_local, "dp") / pack_count
    grad_float = heads_last(grad_arrived.reshape(all_rows, local_width), head_count).astype(
        jnp.float32
    )
    grad_numer = (grad_float / denominator[:, None, :]).astype(jnp.bfloat16)
    grad_denom = -jnp.sum(grad_float * numerator, axis=1) / (denominator * denominator)
    masked_grad = onehot_half[None, :, None, :] * grad_numer[:, None]
    weighted = onehot_float[None, :, :] * grad_denom[:, None, :]
    grad_states = jnp.einsum(
        "hft,hiet->hife", feat_query, masked_grad, preferred_element_type=jnp.float32
    ).astype(jnp.bfloat16)
    grad_totals = jnp.einsum(
        "hft,hit->hif", feat_query.astype(jnp.float32), weighted, precision=highest
    ).astype(jnp.bfloat16)
    grad_fq = jnp.einsum("hiet,hife->hft", masked_grad, states, preferred_element_type=jnp.float32)
    grad_fq = grad_fq + jnp.einsum(
        "hit,hif->hft", weighted, totals.astype(jnp.float32), precision=highest
    )
    gate_query = jnp.where(pre_query > 0, grad_fq, 0.0).astype(jnp.bfloat16)
    grad_queries = (
        jnp.einsum("hft,hef->het", gate_query, omegas, preferred_element_type=jnp.float32)
        * feature_scale
    ).astype(jnp.bfloat16)
    grad_fk = jnp.einsum(
        "hiet,hife->hft", masked_values, grad_states, preferred_element_type=jnp.float32
    )
    grad_fk = grad_fk + jnp.einsum(
        "it,hif->hft", onehot_float, grad_totals.astype(jnp.float32), precision=highest
    )
    gate_key = jnp.where(pre_key > 0, grad_fk, 0.0).astype(jnp.bfloat16)
    grad_keys = (
        jnp.einsum("hft,hef->het", gate_key, omegas, preferred_element_type=jnp.float32)
        * feature_scale
    ).astype(jnp.bfloat16)
    grad_conv = jnp.sum(
        jnp.einsum("hft,hife->hiet", feat_key, grad_states, preferred_element_type=jnp.float32)
        * onehot_float[None, :, None, :],
        axis=1,
    )
    grad_conv = rows_first(grad_conv.astype(jnp.bfloat16))
    grad_queries = rows_first(grad_queries)
    grad_keys = rows_first(grad_keys)
    returned = lax.all_to_all(
        jnp.stack([grad_queries, grad_keys, grad_conv], axis=1).reshape(
            all_rows, 3, 1, local_width
        ),
        "seq",
        split_axis=0,
        concat_axis=2,
        tiled=True,
    )
    returned = returned.reshape(tok_rows, 3, width_all)
    conv_grad_tokens = returned[:, 2]
    padded_grads = with_halo(conv_grad_tokens, (("seq", 0),), margin)
    grad_values = depthwise(padded_grads, margin, rows_local, conv_taps, -1).astype(jnp.bfloat16)
    taps_grad = tap_grads(conv_grad_tokens, padded_values, margin, rows_local)
    grad_tokens = jnp.stack([returned[:, 0], returned[:, 1], grad_values], axis=1)
    gain_sum, taps_sum = lax.psum((pack_gain, taps_grad), ("dp", "seq"))
    return (
        block_sum.astype(jnp.bfloat16)[None],
        grad_tokens[None],
        weight_sum,
        gain_sum / pack_count,
        taps_sum / pack_count,
    )


def solution(mesh):
    in_specs = (
        P("dp", "seq", None, None),
        P("dp", "seq", None),
        P("seq", None),
        P(),
        P(),
        P(),
        P("dp", None, "seq"),
    )
    out_specs = (P("dp", "seq", None), P("dp", "seq", None, None), P("seq", None), P(), P())
    return jax.shard_map(local, mesh=mesh, in_specs=in_specs, out_specs=out_specs, check_vma=False)
```

profile of v0, /device:TPU:1, one launch (start us, length us, event | category | flops | bytes accessed | tf_op | source)
XLA Modules:
  0.0 517.5 jit_solution(8278285979322742595)
XLA Ops:
  9.0 8.8 %collective-permute-start.1 = (bf16[65,1536]{1,0:T(8,128)(2,1)S(1)}, bf16[65,1536]{1,0:T(8,128)(2,1)S(1)}, u32[]{:S(2)}, u32[]{:S(2)}) collective-permute-start(bf16[65,1536]{1,0:T(8,128)(2,1)S(1)} %get-tuple-element.93), channel_id=1, source_target_pairs={{1,0},{2,1},{3,2},{4,3},{5,4},{6,5},{7,6},{8,7},{9,8},{10,9},{11,1... | collective-permute-start | bytes 599048 | tf_op jit(solution)/shard_map/ppermute | solution.py:24
  17.8 1.9 collective-permute-start
  25.5 1.7 gather_fusion.1
  27.1 1.6 gather_fusion.2
  28.8 1.6 gather_fusion.3
  35.3 3.3 fusion.69
  41.0 4.0 all-to-all-start
  45.8 44.2 %all-gather = s32[1,5,2048]{2,0,1:T(1,128)S(1)} all-gather(s32[1,5,128]{2,0,1:T(1,128)S(1)} %copy-done.60), channel_id=2, replica_groups=mesh['dp'=32,'seq'=16] {'seq'}, dimensions={2}, use_global_device_ids=true | all-gather | bytes 43520 | tf_op jit(solution)/shard_map/all_gather | solution.py:102
  91.3 2.5 fusion.32
  93.8 4.5 add_convert_fusion
  103.3 1.9 reduce.27
  106.2 1.8 reshape.592
  108.0 19.7 %all_to_all.63 = bf16[16,2,6144]{2,1,0:T(2,128)(2,1)} all-to-all(bf16[16,2,6144]{2,1,0:T(2,128)(2,1)S(1)} %reshape.592), channel_id=1, replica_groups=mesh['dp'=32,'seq'=16] {'seq'}, dimensions={0} | all-to-all | bytes 786432 | tf_op jit(solution)/shard_map/all_to_all | solution.py:155
  127.7 3.6 reshape.593
  131.3 2.3 copy.149
  135.9 2.3 copy.151
  138.3 4.3 multiply_reduce_fusion
  144.5 4.6 all-to-all-start.2
  151.2 5.1 fusion.31
  157.4 6.1 %all-to-all-done.2 = bf16[128,16,96]{0,2,1:T(8,128)(2,1)S(1)} async-done(((bf16[128,16,96]{0,2,1:T(8,128)(2,1)}), bf16[128,16,96]{0,2,1:T(8,128)(2,1)S(1)}, u32[]{:S(2)}, u32[]{:S(2)}) %all-to-all-start.2) | async-done | bytes 393248 | tf_op jit(solution)/shard_map/all_to_all | solution.py:171
  164.3 4.1 all-to-all-start.4
  170.9 2.2 reshape.368
  173.0 1.6 fusion.85
  174.6 2.5 convolution_convert_fusion.1
  178.3 3.7 fusion.121
  182.1 4.5 fusion.107
  186.7 4.8 fusion.20
  191.5 4.7 fusion.21
  196.3 4.0 fusion.33
  200.4 2.5 copy.156
  203.0 6.3 %all-to-all-start.3 = ((bf16[2048,3,1,96]{3,1,2,0:T(4,128)(2,1)}), bf16[2048,3,1,96]{3,1,2,0:T(4,128)(2,1)}, u32[]{:S(2)}, u32[]{:S(2)}) async-start(bf16[2048,3,1,96]{3,1,2,0:T(4,128)(2,1)} %copy.156), calls=%async_computation.3 | async-start | bytes 4194304 | tf_op jit(solution)/shard_map/all_to_all | solution.py:235
  209.5 1.9 copy.165
  211.5 4.3 fusion.4
  218.3 2.6 fusion.22
  220.9 150.5 %all-reduce.3.cloned.1.call-done = f32[96,1152]{1,0:T(8,128)} async-done(((f32[96,1152]{1,0:T(8,128)}), f32[96,1152]{1,0:T(8,128)}) %all-reduce.3.cloned.1.call-update) | async-done | bytes 442384 | tf_op jit(solution)/shard_map/psum | solution.py:193
  371.4 1.8 broadcast_multiply_fusion
  373.2 2.9 copy.173
  380.6 2.2 fusion.79
  382.8 1.8 fusion.74
  384.8 7.0 %collective-permute-start.3 = (bf16[65,1536]{1,0:T(8,128)(2,1)S(1)}, bf16[65,1536]{1,0:T(8,128)(2,1)S(1)}, u32[]{:S(2)}, u32[]{:S(2)}) collective-permute-start(bf16[65,1536]{1,0:T(8,128)(2,1)S(1)} %bitcast.347), channel_id=1, source_target_pairs={{1,0},{2,1},{3,2},{4,3},{5,4},{6,5},{7,6},{8,7},{9,8},{10,9},{11,1... | collective-permute-start | bytes 599048 | tf_op jit(solution)/shard_map/ppermute | solution.py:24
  392.1 3.0 collective-permute-start.2
  395.3 96.1 %all-reduce = (f32[1536]{0:T(1024)S(1)}, f32[9,1536]{1,0:T(8,128)S(1)}) all-reduce(f32[1536]{0:T(1024)S(1)} %copy-done.58, f32[9,1536]{1,0:T(8,128)S(1)} %stack.64), channel_id=1, replica_groups=mesh['dp'=32,'seq'=16] {'dp','seq'}, use_global_device_ids=true, to_apply=%region_9.11 | all-reduce | flops 15360 | bytes 122880 | tf_op jit(solution)/shard_map/psum | solution.py:250
  496.9 1.8 gather_fusion.10
  498.7 1.8 gather_fusion.17
  500.4 1.8 gather_fusion.15
  502.4 1.8 gather_fusion.11
  504.2 1.8 gather_fusion.9
  506.2 2.8 fusion.103
  (355 shorter events, 48.8 us)
Async XLA Ops:
  7.2 14.9 %copy-start.60 = (s32[1,5,128]{2,0,1:T(1,128)S(1)}, s32[1,5,128]{2,0,1:T(1,128)}, u32[]{:S(2)}) copy-start(s32[1,5,128]{2,0,1:T(1,128)} %param.15) | copy-start | bytes 7684
  7.2 17.0 %copy-start.59 = (f32[9,1536]{1,0:T(8,128)S(1)}, f32[9,1536]{1,0:T(8,128)}, u32[]{:S(2)}) copy-start(f32[9,1536]{1,0:T(8,128)} %param.13) | copy-start | bytes 165892
  7.2 131.1 %all-gather.5.cloned.1.call-start = ((), (), s32[]{:S(2)}) async-start(), calls=%async_computation.5 | async-start | bytes 3760128 | tf_op jit(solution)/shard_map/all_gather | solution.py:161
  9.0 15.4 %collective-permute-start.1 = (bf16[65,1536]{1,0:T(8,128)(2,1)S(1)}, bf16[65,1536]{1,0:T(8,128)(2,1)S(1)}, u32[]{:S(2)}, u32[]{:S(2)}) collective-permute-start(bf16[65,1536]{1,0:T(8,128)(2,1)S(1)} %get-tuple-element.93), channel_id=1, source_target_pairs={{1,0},{2,1},{3,2},{4,3},{5,4},{6,5},{7,6},{8,7},{9,8},{10,9},{11,1... | collective-permute-start | bytes 599048 | tf_op jit(solution)/shard_map/ppermute | solution.py:24
  17.8 6.6 %collective-permute-start = (bf16[65,1536]{1,0:T(8,128)(2,1)S(1)}, bf16[65,1536]{1,0:T(8,128)(2,1)S(1)}, u32[]{:S(2)}, u32[]{:S(2)}) collective-permute-start(bf16[65,1536]{1,0:T(8,128)(2,1)S(1)} %get-tuple-element.92), channel_id=1, source_target_pairs={{0,1},{1,2},{2,3},{3,4},{4,5},{5,6},{6,7},{7,8},{8,9},{9,10},{10,1... | collective-permute-start | bytes 599048 | tf_op jit(solution)/shard_map/ppermute | solution.py:23
  22.1 12.8 %copy-start.100 = (pred[128]{0:T(512)(128)(4,1)}, pred[128]{0:T(512)(128)(4,1)S(1)}, u32[]{:S(2)}) copy-start(pred[128]{0:T(512)(128)(4,1)S(1)} %get-tuple-element.140) | copy-start | bytes 388
  22.1 12.8 %copy-start.103 = (pred[128]{0:T(512)(128)(4,1)}, pred[128]{0:T(512)(128)(4,1)S(1)}, u32[]{:S(2)}) copy-start(pred[128]{0:T(512)(128)(4,1)S(1)} %get-tuple-element.141) | copy-start | bytes 388
  22.8 12.2 %copy-start.66 = (pred[128]{0:T(512)(128)(4,1)}, pred[128]{0:T(512)(128)(4,1)S(1)}, u32[]{:S(2)}) copy-start(pred[128]{0:T(512)(128)(4,1)S(1)} %get-tuple-element.112) | copy-start | bytes 388
  22.8 12.2 %copy-start.68 = (pred[128]{0:T(512)(128)(4,1)}, pred[128]{0:T(512)(128)(4,1)S(1)}, u32[]{:S(2)}) copy-start(pred[128]{0:T(512)(128)(4,1)S(1)} %get-tuple-element.114) | copy-start | bytes 388
  22.8 12.2 %copy-start.70 = (pred[128]{0:T(512)(128)(4,1)}, pred[128]{0:T(512)(128)(4,1)S(1)}, u32[]{:S(2)}) copy-start(pred[128]{0:T(512)(128)(4,1)S(1)} %get-tuple-element.116) | copy-start | bytes 388
  22.8 12.2 %copy-start.72 = (pred[128]{0:T(512)(128)(4,1)}, pred[128]{0:T(512)(128)(4,1)S(1)}, u32[]{:S(2)}) copy-start(pred[128]{0:T(512)(128)(4,1)S(1)} %get-tuple-element.117) | copy-start | bytes 388
  22.8 12.2 %copy-start.109 = (pred[128]{0:T(512)(128)(4,1)}, pred[128]{0:T(512)(128)(4,1)S(1)}, u32[]{:S(2)}) copy-start(pred[128]{0:T(512)(128)(4,1)S(1)} %get-tuple-element.110) | copy-start | bytes 388
  22.8 12.2 %copy-start.111 = (pred[128]{0:T(512)(128)(4,1)}, pred[128]{0:T(512)(128)(4,1)S(1)}, u32[]{:S(2)}) copy-start(pred[128]{0:T(512)(128)(4,1)S(1)} %get-tuple-element.102) | copy-start | bytes 388
  22.9 8.4 %copy-start.97 = (s32[1024]{0:T(1024)}, s32[1024]{0:T(1024)S(1)}, u32[]{:S(2)}) copy-start(s32[1024]{0:T(1024)S(1)} %pad_clamp_fusion.7) | copy-start | bytes 12292
  22.9 12.1 %copy-start.92 = (pred[128]{0:T(512)(128)(4,1)}, pred[128]{0:T(512)(128)(4,1)S(1)}, u32[]{:S(2)}) copy-start(pred[128]{0:T(512)(128)(4,1)S(1)} %get-tuple-element.71) | copy-start | bytes 388
  22.9 12.1 %copy-start.74 = (pred[128]{0:T(512)(128)(4,1)}, pred[128]{0:T(512)(128)(4,1)S(1)}, u32[]{:S(2)}) copy-start(pred[128]{0:T(512)(128)(4,1)S(1)} %get-tuple-element.118) | copy-start | bytes 388
  23.0 12.1 %copy-start.77 = (pred[128]{0:T(512)(128)(4,1)}, pred[128]{0:T(512)(128)(4,1)S(1)}, u32[]{:S(2)}) copy-start(pred[128]{0:T(512)(128)(4,1)S(1)} %get-tuple-element.119) | copy-start | bytes 388
  23.0 12.1 %copy-start.80 = (pred[128]{0:T(512)(128)(4,1)}, pred[128]{0:T(512)(128)(4,1)S(1)}, u32[]{:S(2)}) copy-start(pred[128]{0:T(512)(128)(4,1)S(1)} %get-tuple-element.120) | copy-start | bytes 388
  23.0 12.1 %copy-start.83 = (pred[128]{0:T(512)(128)(4,1)}, pred[128]{0:T(512)(128)(4,1)S(1)}, u32[]{:S(2)}) copy-start(pred[128]{0:T(512)(128)(4,1)S(1)} %get-tuple-element.121) | copy-start | bytes 388
  23.0 12.1 %copy-start.86 = (pred[128]{0:T(512)(128)(4,1)}, pred[128]{0:T(512)(128)(4,1)S(1)}, u32[]{:S(2)}) copy-start(pred[128]{0:T(512)(128)(4,1)S(1)} %get-tuple-element.122) | copy-start | bytes 388
  23.0 12.1 %copy-start.89 = (pred[128]{0:T(512)(128)(4,1)}, pred[128]{0:T(512)(128)(4,1)S(1)}, u32[]{:S(2)}) copy-start(pred[128]{0:T(512)(128)(4,1)S(1)} %get-tuple-element.125) | copy-start | bytes 388
  23.0 12.1 %copy-start.113 = (pred[128]{0:T(512)(128)(4,1)}, pred[128]{0:T(512)(128)(4,1)S(1)}, u32[]{:S(2)}) copy-start(pred[128]{0:T(512)(128)(4,1)S(1)} %get-tuple-element.73) | copy-start | bytes 388
  23.0 12.1 %copy-start.115 = (pred[128]{0:T(512)(128)(4,1)}, pred[128]{0:T(512)(128)(4,1)S(1)}, u32[]{:S(2)}) copy-start(pred[128]{0:T(512)(128)(4,1)S(1)} %get-tuple-element.123) | copy-start | bytes 388
  23.1 10.1 %copy-start.98 = (s32[1024]{0:T(1024)}, s32[1024]{0:T(1024)S(1)}, u32[]{:S(2)}) copy-start(s32[1024]{0:T(1024)S(1)} %get-tuple-element.139) | copy-start | bytes 12292
  24.1 11.0 %copy-start.106 = (pred[128]{0:T(512)(128)(4,1)}, pred[128]{0:T(512)(128)(4,1)S(1)}, u32[]{:S(2)}) copy-start(pred[128]{0:T(512)(128)(4,1)S(1)} %compare_and_fusion.9) | copy-start | bytes 388
  24.3 10.8 %copy-start.38 = (f32[1536]{0:T(1024)}, f32[1536]{0:T(1024)S(1)}, u32[]{:S(2)}) copy-start(f32[1536]{0:T(1024)S(1)} %get-tuple-element.52) | copy-start | bytes 18436
  24.3 10.8 %copy-start.40 = (f32[1536]{0:T(1024)}, f32[1536]{0:T(1024)S(1)}, u32[]{:S(2)}) copy-start(f32[1536]{0:T(1024)S(1)} %get-tuple-element.53) | copy-start | bytes 18436
  24.3 10.8 %copy-start.42 = (f32[1536]{0:T(1024)}, f32[1536]{0:T(1024)S(1)}, u32[]{:S(2)}) copy-start(f32[1536]{0:T(1024)S(1)} %get-tuple-element.54) | copy-start | bytes 18436
  24.3 10.8 %copy-start.44 = (f32[1536]{0:T(1024)}, f32[1536]{0:T(1024)S(1)}, u32[]{:S(2)}) copy-start(f32[1536]{0:T(1024)S(1)} %get-tuple-element.55) | copy-start | bytes 18436
  24.3 10.8 %copy-start.46 = (f32[1536]{0:T(1024)}, f32[1536]{0:T(1024)S(1)}, u32[]{:S(2)}) copy-start(f32[1536]{0:T(1024)S(1)} %get-tuple-element.56) | copy-start | bytes 18436
  24.3 10.8 %copy-start.48 = (f32[1536]{0:T(1024)}, f32[1536]{0:T(1024)S(1)}, u32[]{:S(2)}) copy-start(f32[1536]{0:T(1024)S(1)} %get-tuple-element.57) | copy-start | bytes 18436
  24.4 10.8 %copy-start.50 = (f32[1536]{0:T(1024)}, f32[1536]{0:T(1024)S(1)}, u32[]{:S(2)}) copy-start(f32[1536]{0:T(1024)S(1)} %get-tuple-element.58) | copy-start | bytes 18436
  24.4 10.8 %copy-start.52 = (f32[1536]{0:T(1024)}, f32[1536]{0:T(1024)S(1)}, u32[]{:S(2)}) copy-start(f32[1536]{0:T(1024)S(1)} %get-tuple-element.59) | copy-start | bytes 18436
  24.4 10.8 %copy-start.54 = (f32[1536]{0:T(1024)}, f32[1536]{0:T(1024)S(1)}, u32[]{:S(2)}) copy-start(f32[1536]{0:T(1024)S(1)} %get-tuple-element.60) | copy-start | bytes 18436
  25.5 9.8 %copy-start.6 = (bf16[128,1536]{1,0:T(8,128)(2,1)}, bf16[128,1536]{1,0:T(8,128)(2,1)S(1)}, u32[]{:S(2)}) copy-start(bf16[128,1536]{1,0:T(8,128)(2,1)S(1)} %gather_fusion) | copy-start | bytes 1179652
  39.8 50.2 %copy-start.124 = (s32[48]{0:T(128)S(1)}, s32[48]{0:T(128)}, u32[]{:S(2)}) copy-start(s32[48]{0:T(128)} %param.14) | copy-start | bytes 580
  41.0 49.2 %all-to-all-start = ((bf16[128,3,16,96]{0,3,1,2:T(8,128)(2,1)}), bf16[128,3,16,96]{0,3,1,2:T(8,128)(2,1)S(1)}, u32[]{:S(2)}, u32[]{:S(2)}) async-start(bf16[128,3,16,96]{0,3,1,2:T(8,128)(2,1)} %copy.146), calls=%async_computation | async-start | bytes 2359296 | tf_op jit(solution)/shard_map/all_to_all | solution.py:106
  45.0 166.4 %all-gather.7.cloned.1.call-start = ((), (), s32[]{:S(2)}) async-start(), calls=%async_computation.7 | async-start | bytes 5013504 | tf_op jit(solution)/shard_map/all_gather | solution.py:190
  90.1 9.1 %copy-start.61 = (bf16[3,2048]{1,0:T(4,128)(2,1)}, bf16[3,2048]{1,0:T(4,128)(2,1)S(1)}, u32[]{:S(2)}) copy-start(bf16[3,2048]{1,0:T(4,128)(2,1)S(1)} %get-tuple-element.97) | copy-start | bytes 36868
  90.2 10.9 %copy-start.17 = (f32[3,2048]{1,0:T(4,128)}, f32[3,2048]{1,0:T(4,128)S(1)}, u32[]{:S(2)}) copy-start(f32[3,2048]{1,0:T(4,128)S(1)} %get-tuple-element.96) | copy-start | bytes 73732
  144.5 19.0 %all-to-all-start.2 = ((bf16[128,16,96]{0,2,1:T(8,128)(2,1)}), bf16[128,16,96]{0,2,1:T(8,128)(2,1)S(1)}, u32[]{:S(2)}, u32[]{:S(2)}) async-start(bf16[128,16,96]{0,2,1:T(8,128)(2,1)} %bitcast.34), calls=%async_computation.2 | async-start | bytes 786432 | tf_op jit(solution)/shard_map/all_to_all | solution.py:171
  164.3 38.7 %all-to-all-start.4 = ((bf16[128,16,96]{0,2,1:T(8,128)(2,1)}), bf16[128,16,96]{0,2,1:T(8,128)(2,1)}, u32[]{:S(2)}, u32[]{:S(2)}) async-start(bf16[128,16,96]{0,2,1:T(8,128)(2,1)} %copy.164), calls=%async_computation.4 | async-start | bytes 786432 | tf_op jit(solution)/shard_map/all_to_all | solution.py:178
  203.0 170.2 %all-to-all-start.3 = ((bf16[2048,3,1,96]{3,1,2,0:T(4,128)(2,1)}), bf16[2048,3,1,96]{3,1,2,0:T(4,128)(2,1)}, u32[]{:S(2)}, u32[]{:S(2)}) async-start(bf16[2048,3,1,96]{3,1,2,0:T(4,128)(2,1)} %copy.156), calls=%async_computation.3 | async-start | bytes 4194304 | tf_op jit(solution)/shard_map/all_to_all | solution.py:235
  209.3 162.1 %all-reduce.3.cloned.1.call-start = ((), (), s32[]{:S(2)}) async-start(), calls=%async_computation.6 | async-start | bytes 884736 | tf_op jit(solution)/shard_map/psum | solution.py:193
  379.1 12.7 %copy-start.21 = (bf16[65,1,1536]{0,2,1:T(8,128)(2,1)S(1)}, bf16[65,1,1536]{0,2,1:T(8,128)(2,1)}, u32[]{:S(2)}) copy-start(bf16[65,1,1536]{0,2,1:T(8,128)(2,1)} %get-tuple-element.87) | copy-start | bytes 599044
  380.6 14.7 %copy-start.58 = (f32[1536]{0:T(1024)S(1)}, f32[1536]{0:T(1024)}, u32[]{:S(2)}) copy-start(f32[1536]{0:T(1024)} %get-tuple-element.41) | copy-start | bytes 18436
  384.8 107.9 %collective-permute-start.3 = (bf16[65,1536]{1,0:T(8,128)(2,1)S(1)}, bf16[65,1536]{1,0:T(8,128)(2,1)S(1)}, u32[]{:S(2)}, u32[]{:S(2)}) collective-permute-start(bf16[65,1536]{1,0:T(8,128)(2,1)S(1)} %bitcast.347), channel_id=1, source_target_pairs={{1,0},{2,1},{3,2},{4,3},{5,4},{6,5},{7,6},{8,7},{9,8},{10,9},{11,1... | collective-permute-start | bytes 599048 | tf_op jit(solution)/shard_map/ppermute | solution.py:24
  392.1 100.6 %collective-permute-start.2 = (bf16[65,1536]{1,0:T(8,128)(2,1)S(1)}, bf16[65,1536]{1,0:T(8,128)(2,1)S(1)}, u32[]{:S(2)}, u32[]{:S(2)}) collective-permute-start(bf16[65,1536]{1,0:T(8,128)(2,1)S(1)} %bitcast.348), channel_id=1, source_target_pairs={{0,1},{1,2},{2,3},{3,4},{4,5},{5,6},{6,7},{7,8},{8,9},{9,10},{10,1... | collective-permute-start | bytes 599048 | tf_op jit(solution)/shard_map/ppermute | solution.py:23
  (88 other events, 373.2 us)
Sparse Core Ops, SparseCore 0:
  10.1 62.2 all-gather.4
  74.6 53.0 all-gather.6
  215.9 155.4 all-reduce.2
where the time goes:
time: 524 us; the launch traced here: 518 us
  blocking collectives  160 us (31%)
  waiting for transfers between devices  158 us (30%)
  local copies, waits for them, and re-layouts  67.4 us (13%)
  matrix products  46.9 us (9%)
  starting transfers between devices  40.1 us (8%)
  other arithmetic  28.9 us (6%)
  between operations  16.1 us (3%)
    psum x1, waiting for transfers between devices, local(): weight_sum = lax.psum(weight_local, 'dp') / pack_count  151 us
    psum x1, blocking collectives, local(): gain_sum, taps_sum = lax.psum((pack_gain, taps_grad), ('dp', 'seq'))  96.1 us
    all_gather x1, blocking collectives, local(): rows_all = lax.all_gather(rows_local, 'seq', axis=1, tiled=True)  44.2 us
    gather x18, local copies, waits for them, and re-layouts, neighbour(): jnp.take(padded, source, axis=0)  23.2 us
    all_to_all x1, blocking collectives, local(): lax.all_to_all(attention_heads, 'seq', split_axis=0, concat_axis=1, tiled...  19.7 us
    ppermute x2, starting transfers between devices, with_halo(): after = lax.ppermute(initial, axis, down)  15.8 us
    unnamed x258, local copies, waits for them, and re-layouts  12.1 us
  transfers between devices with their start and end apart: 11, of which 2 were waited for; matrix products, arithmetic and copies ran while one was open for 22% of the time, Pallas kernels for 0%

commit v1 on v0

--- a/solution.py
+++ b/solution.py
@@ -190,7 +190,7 @@
         lax.all_gather(grad_in, "seq", axis=0, tiled=True),
         preferred_element_type=jnp.float32,
     )
-    weight_sum = lax.psum(weight_local, "dp") / pack_count
+    weight_sum = jnp.sum(lax.all_gather(weight_local, "dp"), axis=0) / pack_count
     grad_float = heads_last(grad_arrived.reshape(all_rows, local_width), head_count).astype(
         jnp.float32
     )

time: 524 us -> 437 us (0.83)
  waiting for transfers between devices: 158 us -> 65.9 us
  other arithmetic: 28.9 us -> 35.1 us
  starting transfers between devices: 40.1 us -> 34.7 us
    psum x1 -> x0, waiting for transfers between devices: 151 us -> none  [local(): weight_sum = lax.psum(weight_local, 'dp') / pack_count]
    all_to_all x1, waiting for transfers between devices: 0.01 us -> 42.8 us  [local(): lax.all_to_all(jnp.stack([grad_queries, grad_keys, grad_conv], axis=1).re...]
    all_to_all x1, waiting for transfers between devices: 0.01 us -> 12.9 us  [local(): lax.all_to_all(attention_heads, 'seq', split_axis=0, concat_axis=1, tiled...]
    reduce_sum x0 -> x1, other arithmetic: none -> 5.69 us  [local(): jnp.sum(lax.all_gather(weight_local, 'dp'), axis=0) / pack_count]
    unnamed x258 -> x264, local copies, waits for them, and re-layouts: 12.1 us -> 14.3 us
  transfers between devices with their start and end apart: 11 -> 11, of which waited for: 2 -> 3; matrix products, arithmetic and copies ran while one was open for 22% -> 33% of each run, Pallas kernels for 0% -> 0%
where the time goes in v1:
time: 437 us; the launch traced here: 430 us
  blocking collectives  165 us (38%)
  local copies, waits for them, and re-layouts  70.1 us (16%)
  waiting for transfers between devices  65.9 us (15%)
  matrix products  43.5 us (10%)
  other arithmetic  35.1 us (8%)
  starting transfers between devices  34.7 us (8%)
  between operations  16.1 us (4%)
    psum x1, blocking collectives, local(): gain_sum, taps_sum = lax.psum((pack_gain, taps_grad), ('dp', 'seq'))  99.6 us
    all_gather x1, blocking collectives, local(): rows_all = lax.all_gather(rows_local, 'seq', axis=1, tiled=True)  46.6 us
    all_to_all x1, waiting for transfers between devices, local(): lax.all_to_all(jnp.stack([grad_queries, grad_keys, grad_conv], axis=1).re...  42.8 us
    gather x18, local copies, waits for them, and re-layouts, neighbour(): jnp.take(padded, source, axis=0)  23.3 us
    all_to_all x1, blocking collectives, local(): lax.all_to_all(normed.reshape(tok_rows, groups, local_width), 'seq', spli...  18.8 us
    unnamed x264, local copies, waits for them, and re-layouts  14.3 us
    all_to_all x1, waiting for transfers between devices, local(): lax.all_to_all(attention_heads, 'seq', split_axis=0, concat_axis=1, tiled...  12.9 us
    ppermute x2, starting transfers between devices, with_halo(): after = lax.ppermute(initial, axis, down)  11.3 us
  transfers between devices with their start and end apart: 11, of which 3 were waited for; matrix products, arithmetic and copies ran while one was open for 33% of the time, Pallas kernels for 0%

profile of v1, /device:TPU:1, one launch (start us, length us, event | category | flops | bytes accessed | tf_op | source)
XLA Modules:
  0.0 430.3 jit_solution(10221225819187990218)
XLA Ops:
  9.0 8.8 %collective-permute-start.1 = (bf16[65,1536]{1,0:T(8,128)(2,1)S(1)}, bf16[65,1536]{1,0:T(8,128)(2,1)S(1)}, u32[]{:S(2)}, u32[]{:S(2)}) collective-permute-start(bf16[65,1536]{1,0:T(8,128)(2,1)S(1)} %get-tuple-element.93), channel_id=1, source_target_pairs={{1,0},{2,1},{3,2},{4,3},{5,4},{6,5},{7,6},{8,7},{9,8},{10,9},{11,1... | collective-permute-start | bytes 599048 | tf_op jit(solution)/shard_map/ppermute | solution.py:24
  17.8 1.9 collective-permute-start
  25.5 1.7 gather_fusion.1
  27.1 1.7 gather_fusion.2
  28.8 1.7 gather_fusion.3
  35.3 3.3 fusion.69
  41.1 4.0 all-to-all-start
  46.0 46.6 %all-gather = s32[1,5,2048]{2,0,1:T(1,128)S(1)} all-gather(s32[1,5,128]{2,0,1:T(1,128)S(1)} %copy-done.59), channel_id=2, replica_groups=mesh['dp'=32,'seq'=16] {'seq'}, dimensions={2}, use_global_device_ids=true | all-gather | bytes 43520 | tf_op jit(solution)/shard_map/all_gather | solution.py:102
  93.8 2.5 fusion.32
  97.2 4.0 add_convert_fusion
  105.8 1.9 reduce.27
  108.7 2.6 reshape.593
  111.3 5.3 %all-to-all-start.1 = ((bf16[16,2,6144]{2,1,0:T(2,128)(2,1)}), bf16[16,2,6144]{2,1,0:T(2,128)(2,1)S(1)}, u32[]{:S(2)}, u32[]{:S(2)}) async-start(bf16[16,2,6144]{2,1,0:T(2,128)(2,1)} %reshape.593), calls=%async_computation.1 | async-start | bytes 786432 | tf_op jit(solution)/shard_map/all_to_all | solution.py:155
  118.8 12.9 %all-to-all-done.1 = bf16[16,2,6144]{2,1,0:T(2,128)(2,1)S(1)} async-done(((bf16[16,2,6144]{2,1,0:T(2,128)(2,1)}), bf16[16,2,6144]{2,1,0:T(2,128)(2,1)S(1)}, u32[]{:S(2)}, u32[]{:S(2)}) %all-to-all-start.1) | async-done | bytes 393248 | tf_op jit(solution)/shard_map/all_to_all | solution.py:155
  131.6 2.0 reshape.594
  133.6 2.3 copy.149
  137.4 18.8 %all_to_all.63 = bf16[128,16,96]{0,2,1:T(8,128)(2,1)S(1)} all-to-all(bf16[128,16,96]{0,2,1:T(8,128)(2,1)S(1)} %copy.164), channel_id=1, replica_groups=mesh['dp'=32,'seq'=16] {'seq'}, dimensions={1} | all-to-all | bytes 786432 | tf_op jit(solution)/shard_map/all_to_all | solution.py:178
  156.4 4.0 fusion.4
  160.4 2.3 copy.150
  162.7 2.3 copy.151
  165.0 4.2 multiply_reduce_fusion
  171.1 4.3 all-to-all-start.2
  175.4 5.0 %fusion.31 = u8[256,2048]{1,0:T(8,128)(4,1)} fusion(f32[3,256,2048]{2,1,0:T(8,128)} %get-tuple-element.128), kind=kLoop, calls=%fused_computation.63 | loop fusion | flops 8912896 | bytes 6815744
  180.4 8.8 %all-to-all-done.2 = bf16[128,16,96]{0,2,1:T(8,128)(2,1)} async-done(((bf16[128,16,96]{0,2,1:T(8,128)(2,1)}), bf16[128,16,96]{0,2,1:T(8,128)(2,1)}, u32[]{:S(2)}, u32[]{:S(2)}) %all-to-all-start.2) | async-done | bytes 393248 | tf_op jit(solution)/shard_map/all_to_all | solution.py:171
  191.6 2.2 reshape.368
  195.4 2.5 convolution_convert_fusion.1
  199.1 3.7 fusion.121
  202.8 4.6 %fusion.107 = f32[3,256,2048]{2,1,0:T(8,128)} fusion(bf16[3,3,256]{2,1,0:T(4,128)(2,1)S(1)} %copy-done.56, f32[3,2048]{1,0:T(4,128)S(1)} %multiply_divide_fusion, f32[3,2048]{1,0:T(4,128)S(1)} %copy-done.19), kind=kOutput, calls=%fused_computation.167 | convolution fusion | flops 56641536 | bytes 6345216 | tf_op jit(solution)/shard_map/hit,hif->hft/dot_general | solution.py:208
  208.8 4.8 %fusion.21 = bf16[3,32,2048]{2,1,0:T(8,128)(2,1)S(1)} fusion(f32[3,256,2048]{2,1,0:T(8,128)} %fusion.121, bf16[3,3,256,32]{2,3,1,0:T(8,128)(2,1)S(1)} %fusion.54, u8[256,2048]{1,0:T(8,128)(4,1)S(1)} %copy-done.25, bf16[3,32,2048]{2,1,0:T(8,128)(2,1)S(1)} %bitcast.349, bf16[3,2048]{1,0:T(4,128)(2,1)S(1)} %copy-done.61, s32[32,256]{1,0:T(8,128)S(1)} %copy-done.32, ...), kind=kOutput, calls=%fused_computation.56 | convolution fusion | flops 415113216 | bytes 7794700 | tf_op jit(solution)/shard_map/hft,hef->het/dot_general | solution.py:224
  213.6 4.9 %fusion.20 = bf16[3,32,2048]{2,1,0:T(8,128)(2,1)S(1)} fusion(f32[3,256,2048]{2,1,0:T(8,128)} %fusion.107, bf16[3,3,256,32]{2,3,1,0:T(8,128)(2,1)S(1)} %copy-done.35, u8[256,2048]{1,0:T(8,128)(4,1)S(1)} %copy-done.26, bf16[3,32,2048]{2,1,0:T(8,128)(2,1)S(1)} %copy-done.30, bf16[3,2048]{1,0:T(4,128)(2,1)S(1)} %copy-done.61, s32[32,256]{1,0:T(8,128)S(1)} %copy-done.32, ...), kind=kOutput, calls=%fused_computation.55 | convolution fusion | flops 415113216 | bytes 7794700 | tf_op jit(solution)/shard_map/hft,hef->het/dot_general | solution.py:213
  219.7 4.2 copy.156
  224.0 4.6 %all-to-all-start.3 = ((bf16[2048,3,1,96]{3,1,2,0:T(4,128)(2,1)}), bf16[2048,3,1,96]{3,1,2,0:T(4,128)(2,1)}, u32[]{:S(2)}, u32[]{:S(2)}) async-start(bf16[2048,3,1,96]{3,1,2,0:T(4,128)(2,1)} %copy.156), calls=%async_computation.3 | async-start | bytes 4194304 | tf_op jit(solution)/shard_map/all_to_all | solution.py:235
  231.0 2.6 fusion.22
  233.6 42.8 %all-to-all-done.3 = bf16[2048,3,1,96]{3,1,2,0:T(4,128)(2,1)} async-done(((bf16[2048,3,1,96]{3,1,2,0:T(4,128)(2,1)}), bf16[2048,3,1,96]{3,1,2,0:T(4,128)(2,1)}, u32[]{:S(2)}, u32[]{:S(2)}) %all-to-all-start.3) | async-done | bytes 1179680 | tf_op jit(solution)/shard_map/all_to_all | solution.py:235
  276.4 3.0 copy.173
  282.3 2.0 copy.176
  284.3 2.5 collective-permute-start.3
  288.0 1.9 copy.174
  289.9 3.2 collective-permute-start.2
  293.2 2.2 fusion.79
  297.3 99.6 %all-reduce = (f32[1536]{0:T(1024)S(1)}, f32[9,1536]{1,0:T(8,128)S(1)}) all-reduce(f32[1536]{0:T(1024)S(1)} %copy-done.57, f32[9,1536]{1,0:T(8,128)S(1)} %stack.64), channel_id=1, replica_groups=mesh['dp'=32,'seq'=16] {'dp','seq'}, use_global_device_ids=true, to_apply=%region_9.11 | all-reduce | flops 15360 | bytes 122880 | tf_op jit(solution)/shard_map/psum | solution.py:250
  403.2 1.8 gather_fusion.10
  405.0 1.8 gather_fusion.17
  406.8 1.7 gather_fusion.15
  408.7 1.8 gather_fusion.11
  410.5 1.8 gather_fusion.9
  412.5 2.8 fusion.103
  417.1 5.7 %reduce_sum.171 = f32[96,1152]{1,0:T(8,128)S(1)} reduce(f32[32,96,1152]{2,1,0:T(8,128)} %bitcast.328, f32[]{:T(128)} %constant.82.clone.1), dimensions={0}, to_apply=%region_7.9 | reduce | flops 3428352 | bytes 14598148 | tf_op jit(solution)/shard_map/reduce_sum | solution.py:193
  (363 shorter events, 53.0 us)
Async XLA Ops:
  7.2 14.9 %copy-start.59 = (s32[1,5,128]{2,0,1:T(1,128)S(1)}, s32[1,5,128]{2,0,1:T(1,128)}, u32[]{:S(2)}) copy-start(s32[1,5,128]{2,0,1:T(1,128)} %param.15) | copy-start | bytes 7684
  7.2 16.9 %copy-start.58 = (f32[9,1536]{1,0:T(8,128)S(1)}, f32[9,1536]{1,0:T(8,128)}, u32[]{:S(2)}) copy-start(f32[9,1536]{1,0:T(8,128)} %param.13) | copy-start | bytes 165892
  7.2 149.2 %all-gather.9.cloned.1.call-start = ((), (), s32[]{:S(2)}) async-start(), calls=%async_computation.6 | async-start | bytes 5013504 | tf_op jit(solution)/shard_map/all_gather | solution.py:190
  9.0 15.4 %collective-permute-start.1 = (bf16[65,1536]{1,0:T(8,128)(2,1)S(1)}, bf16[65,1536]{1,0:T(8,128)(2,1)S(1)}, u32[]{:S(2)}, u32[]{:S(2)}) collective-permute-start(bf16[65,1536]{1,0:T(8,128)(2,1)S(1)} %get-tuple-element.93), channel_id=1, source_target_pairs={{1,0},{2,1},{3,2},{4,3},{5,4},{6,5},{7,6},{8,7},{9,8},{10,9},{11,1... | collective-permute-start | bytes 599048 | tf_op jit(solution)/shard_map/ppermute | solution.py:24
  17.8 6.6 %collective-permute-start = (bf16[65,1536]{1,0:T(8,128)(2,1)S(1)}, bf16[65,1536]{1,0:T(8,128)(2,1)S(1)}, u32[]{:S(2)}, u32[]{:S(2)}) collective-permute-start(bf16[65,1536]{1,0:T(8,128)(2,1)S(1)} %get-tuple-element.92), channel_id=1, source_target_pairs={{0,1},{1,2},{2,3},{3,4},{4,5},{5,6},{6,7},{7,8},{8,9},{9,10},{10,1... | collective-permute-start | bytes 599048 | tf_op jit(solution)/shard_map/ppermute | solution.py:23
  22.1 12.9 %copy-start.99 = (pred[128]{0:T(512)(128)(4,1)}, pred[128]{0:T(512)(128)(4,1)S(1)}, u32[]{:S(2)}) copy-start(pred[128]{0:T(512)(128)(4,1)S(1)} %get-tuple-element.140) | copy-start | bytes 388
  22.1 12.9 %copy-start.102 = (pred[128]{0:T(512)(128)(4,1)}, pred[128]{0:T(512)(128)(4,1)S(1)}, u32[]{:S(2)}) copy-start(pred[128]{0:T(512)(128)(4,1)S(1)} %get-tuple-element.141) | copy-start | bytes 388
  22.8 12.3 %copy-start.69 = (pred[128]{0:T(512)(128)(4,1)}, pred[128]{0:T(512)(128)(4,1)S(1)}, u32[]{:S(2)}) copy-start(pred[128]{0:T(512)(128)(4,1)S(1)} %get-tuple-element.116) | copy-start | bytes 388
  22.8 12.3 %copy-start.71 = (pred[128]{0:T(512)(128)(4,1)}, pred[128]{0:T(512)(128)(4,1)S(1)}, u32[]{:S(2)}) copy-start(pred[128]{0:T(512)(128)(4,1)S(1)} %get-tuple-element.117) | copy-start | bytes 388
  41.1 51.5 %all-to-all-start = ((bf16[128,3,16,96]{0,3,1,2:T(8,128)(2,1)}), bf16[128,3,16,96]{0,3,1,2:T(8,128)(2,1)S(1)}, u32[]{:S(2)}, u32[]{:S(2)}) async-start(bf16[128,3,16,96]{0,3,1,2:T(8,128)(2,1)} %copy.146), calls=%async_computation | async-start | bytes 2359296 | tf_op jit(solution)/shard_map/all_to_all | solution.py:106
  45.1 119.9 %all-gather.7.cloned.1.call-start = ((), (), s32[]{:S(2)}) async-start(), calls=%async_computation.5 | async-start | bytes 3760128 | tf_op jit(solution)/shard_map/all_gather | solution.py:161
  46.0 51.2 %copy-start.116 = (s32[3]{0:T(128)}, s32[3]{0:T(128)S(1)}, u32[]{:S(2)}) copy-start(s32[3]{0:T(128)S(1)} %dynamic-slice_multiply_fusion) | copy-start | bytes 40
  103.6 13.1 %copy-start.36 = (f32[1536]{0:T(1024)S(1)}, f32[1536]{0:T(1024)}, u32[]{:S(2)}) copy-start(f32[1536]{0:T(1024)} %param.12) | copy-start | bytes 18436
  111.3 20.3 %all-to-all-start.1 = ((bf16[16,2,6144]{2,1,0:T(2,128)(2,1)}), bf16[16,2,6144]{2,1,0:T(2,128)(2,1)S(1)}, u32[]{:S(2)}, u32[]{:S(2)}) async-start(bf16[16,2,6144]{2,1,0:T(2,128)(2,1)} %reshape.593), calls=%async_computation.1 | async-start | bytes 786432 | tf_op jit(solution)/shard_map/all_to_all | solution.py:155
  116.7 300.4 %all-gather.11.cloned.1.call-start = ((), (), s32[]{:S(2)}) async-start(), calls=%async_computation.7 | async-start | bytes 14598144 | tf_op jit(solution)/shard_map/all_gather | solution.py:193
  137.0 19.1 %copy-start.62 = (f32[128]{0:T(128)}, f32[128]{0:T(128)S(1)}, u32[]{:S(2)}) copy-start(f32[128]{0:T(128)S(1)} %add_rsqrt_fusion) | copy-start | bytes 1540
  171.1 18.1 %all-to-all-start.2 = ((bf16[128,16,96]{0,2,1:T(8,128)(2,1)}), bf16[128,16,96]{0,2,1:T(8,128)(2,1)}, u32[]{:S(2)}, u32[]{:S(2)}) async-start(bf16[128,16,96]{0,2,1:T(8,128)(2,1)} %bitcast.34), calls=%async_computation.2 | async-start | bytes 786432 | tf_op jit(solution)/shard_map/all_to_all | solution.py:171
  180.4 13.4 %copy-start.24 = (f32[3,2048]{1,0:T(4,128)S(1)}, f32[3,2048]{1,0:T(4,128)}, u32[]{:S(2)}) copy-start(f32[3,2048]{1,0:T(4,128)} %copy-done.23) | copy-start | bytes 73732
  180.4 15.0 %copy-start.19 = (f32[3,2048]{1,0:T(4,128)S(1)}, f32[3,2048]{1,0:T(4,128)}, u32[]{:S(2)}) copy-start(f32[3,2048]{1,0:T(4,128)} %copy-done.18) | copy-start | bytes 73732
  224.0 52.5 %all-to-all-start.3 = ((bf16[2048,3,1,96]{3,1,2,0:T(4,128)(2,1)}), bf16[2048,3,1,96]{3,1,2,0:T(4,128)(2,1)}, u32[]{:S(2)}, u32[]{:S(2)}) async-start(bf16[2048,3,1,96]{3,1,2,0:T(4,128)(2,1)} %copy.156), calls=%async_computation.3 | async-start | bytes 4194304 | tf_op jit(solution)/shard_map/all_to_all | solution.py:235
  279.4 13.7 %copy-start.6 = (bf16[128,1536]{1,0:T(8,128)(2,1)S(1)}, bf16[128,1536]{1,0:T(8,128)(2,1)}, u32[]{:S(2)}) copy-start(bf16[128,1536]{1,0:T(8,128)(2,1)} %copy-done.5) | copy-start | bytes 1179652
  279.4 13.7 %copy-start.8 = (bf16[128,1536]{1,0:T(8,128)(2,1)S(1)}, bf16[128,1536]{1,0:T(8,128)(2,1)}, u32[]{:S(2)}) copy-start(bf16[128,1536]{1,0:T(8,128)(2,1)} %copy-done.7) | copy-start | bytes 1179652
  279.4 13.7 %copy-start.10 = (bf16[128,1536]{1,0:T(8,128)(2,1)S(1)}, bf16[128,1536]{1,0:T(8,128)(2,1)}, u32[]{:S(2)}) copy-start(bf16[128,1536]{1,0:T(8,128)(2,1)} %copy-done.9) | copy-start | bytes 1179652
  279.4 13.7 %copy-start.12 = (bf16[128,1536]{1,0:T(8,128)(2,1)S(1)}, bf16[128,1536]{1,0:T(8,128)(2,1)}, u32[]{:S(2)}) copy-start(bf16[128,1536]{1,0:T(8,128)(2,1)} %copy-done.11) | copy-start | bytes 1179652
  279.4 13.7 %copy-start.14 = (bf16[128,1536]{1,0:T(8,128)(2,1)S(1)}, bf16[128,1536]{1,0:T(8,128)(2,1)}, u32[]{:S(2)}) copy-start(bf16[128,1536]{1,0:T(8,128)(2,1)} %copy-done.13) | copy-start | bytes 1179652
  279.4 13.7 %copy-start.72 = (pred[128]{0:T(512)(128)(4,1)S(1)}, pred[128]{0:T(512)(128)(4,1)}, u32[]{:S(2)}) copy-start(pred[128]{0:T(512)(128)(4,1)} %copy-done.71) | copy-start | bytes 388
  279.5 13.7 %copy-start.74 = (pred[128]{0:T(512)(128)(4,1)S(1)}, pred[128]{0:T(512)(128)(4,1)}, u32[]{:S(2)}) copy-start(pred[128]{0:T(512)(128)(4,1)} %copy-done.73) | copy-start | bytes 388
  279.5 13.7 %copy-start.80 = (pred[128]{0:T(512)(128)(4,1)S(1)}, pred[128]{0:T(512)(128)(4,1)}, u32[]{:S(2)}) copy-start(pred[128]{0:T(512)(128)(4,1)} %copy-done.79) | copy-start | bytes 388
  279.5 13.7 %copy-start.83 = (pred[128]{0:T(512)(128)(4,1)S(1)}, pred[128]{0:T(512)(128)(4,1)}, u32[]{:S(2)}) copy-start(pred[128]{0:T(512)(128)(4,1)} %copy-done.82) | copy-start | bytes 388
  279.5 13.7 %copy-start.86 = (pred[128]{0:T(512)(128)(4,1)S(1)}, pred[128]{0:T(512)(128)(4,1)}, u32[]{:S(2)}) copy-start(pred[128]{0:T(512)(128)(4,1)} %copy-done.85) | copy-start | bytes 388
  279.5 13.7 %copy-start.89 = (pred[128]{0:T(512)(128)(4,1)S(1)}, pred[128]{0:T(512)(128)(4,1)}, u32[]{:S(2)}) copy-start(pred[128]{0:T(512)(128)(4,1)} %copy-done.88) | copy-start | bytes 388
  279.5 13.7 %copy-start.92 = (pred[128]{0:T(512)(128)(4,1)S(1)}, pred[128]{0:T(512)(128)(4,1)}, u32[]{:S(2)}) copy-start(pred[128]{0:T(512)(128)(4,1)} %copy-done.91) | copy-start | bytes 388
  279.5 13.7 %copy-start.100 = (pred[128]{0:T(512)(128)(4,1)S(1)}, pred[128]{0:T(512)(128)(4,1)}, u32[]{:S(2)}) copy-start(pred[128]{0:T(512)(128)(4,1)} %copy-done.99) | copy-start | bytes 388
  279.5 13.7 %copy-start.103 = (pred[128]{0:T(512)(128)(4,1)S(1)}, pred[128]{0:T(512)(128)(4,1)}, u32[]{:S(2)}) copy-start(pred[128]{0:T(512)(128)(4,1)} %copy-done.102) | copy-start | bytes 388
  279.5 13.7 %copy-start.111 = (pred[128]{0:T(512)(128)(4,1)S(1)}, pred[128]{0:T(512)(128)(4,1)}, u32[]{:S(2)}) copy-start(pred[128]{0:T(512)(128)(4,1)} %copy-done.110) | copy-start | bytes 388
  279.5 13.7 %copy-start.113 = (pred[128]{0:T(512)(128)(4,1)S(1)}, pred[128]{0:T(512)(128)(4,1)}, u32[]{:S(2)}) copy-start(pred[128]{0:T(512)(128)(4,1)} %copy-done.112) | copy-start | bytes 388
  279.6 13.7 %copy-start.115 = (pred[128]{0:T(512)(128)(4,1)S(1)}, pred[128]{0:T(512)(128)(4,1)}, u32[]{:S(2)}) copy-start(pred[128]{0:T(512)(128)(4,1)} %copy-done.114) | copy-start | bytes 388
  281.3 14.2 %copy-start.66 = (pred[128]{0:T(512)(128)(4,1)S(1)}, pred[128]{0:T(512)(128)(4,1)}, u32[]{:S(2)}) copy-start(pred[128]{0:T(512)(128)(4,1)} %copy-done.65) | copy-start | bytes 388
  281.3 14.2 %copy-start.68 = (pred[128]{0:T(512)(128)(4,1)S(1)}, pred[128]{0:T(512)(128)(4,1)}, u32[]{:S(2)}) copy-start(pred[128]{0:T(512)(128)(4,1)} %copy-done.67) | copy-start | bytes 388
  281.3 14.2 %copy-start.70 = (pred[128]{0:T(512)(128)(4,1)S(1)}, pred[128]{0:T(512)(128)(4,1)}, u32[]{:S(2)}) copy-start(pred[128]{0:T(512)(128)(4,1)} %copy-done.69) | copy-start | bytes 388
  281.3 14.2 %copy-start.77 = (pred[128]{0:T(512)(128)(4,1)S(1)}, pred[128]{0:T(512)(128)(4,1)}, u32[]{:S(2)}) copy-start(pred[128]{0:T(512)(128)(4,1)} %copy-done.76) | copy-start | bytes 388
  281.3 14.2 %copy-start.106 = (pred[128]{0:T(512)(128)(4,1)S(1)}, pred[128]{0:T(512)(128)(4,1)}, u32[]{:S(2)}) copy-start(pred[128]{0:T(512)(128)(4,1)} %copy-done.105) | copy-start | bytes 388
  281.3 14.2 %copy-start.109 = (pred[128]{0:T(512)(128)(4,1)S(1)}, pred[128]{0:T(512)(128)(4,1)}, u32[]{:S(2)}) copy-start(pred[128]{0:T(512)(128)(4,1)} %copy-done.108) | copy-start | bytes 388
  282.3 13.2 %copy-start.16 = (bf16[128,1536]{1,0:T(8,128)(2,1)S(1)}, bf16[128,1536]{1,0:T(8,128)(2,1)}, u32[]{:S(2)}) copy-start(bf16[128,1536]{1,0:T(8,128)(2,1)} %gather_fusion.1) | copy-start | bytes 1179652
  282.3 13.2 %copy-start.17 = (bf16[128,1536]{1,0:T(8,128)(2,1)S(1)}, bf16[128,1536]{1,0:T(8,128)(2,1)}, u32[]{:S(2)}) copy-start(bf16[128,1536]{1,0:T(8,128)(2,1)} %gather_fusion.2) | copy-start | bytes 1179652
  284.3 12.9 %copy-start.57 = (f32[1536]{0:T(1024)S(1)}, f32[1536]{0:T(1024)}, u32[]{:S(2)}) copy-start(f32[1536]{0:T(1024)} %get-tuple-element.41) | copy-start | bytes 18436
  284.3 113.7 %collective-permute-start.3 = (bf16[65,1536]{1,0:T(8,128)(2,1)}, bf16[65,1536]{1,0:T(8,128)(2,1)S(1)}, u32[]{:S(2)}, u32[]{:S(2)}) collective-permute-start(bf16[65,1536]{1,0:T(8,128)(2,1)} %bitcast.60), channel_id=1, source_target_pairs={{1,0},{2,1},{3,2},{4,3},{5,4},{6,5},{7,6},{8,7},{9,8},{10,9},{11,1... | collective-permute-start | bytes 599048 | tf_op jit(solution)/shard_map/ppermute | solution.py:24
  289.9 108.2 %collective-permute-start.2 = (bf16[65,1536]{1,0:T(8,128)(2,1)}, bf16[65,1536]{1,0:T(8,128)(2,1)}, u32[]{:S(2)}, u32[]{:S(2)}) collective-permute-start(bf16[65,1536]{1,0:T(8,128)(2,1)} %bitcast.352), channel_id=1, source_target_pairs={{0,1},{1,2},{2,3},{3,4},{4,5},{5,6},{6,7},{7,8},{8,9},{9,10},{10,1... | collective-permute-start | bytes 599048 | tf_op jit(solution)/shard_map/ppermute | solution.py:23
  (91 other events, 585.9 us)
Sparse Core Ops, SparseCore 0:
  10.1 73.7 all-gather.8
  86.0 46.8 all-gather.6
  160.5 130.1 all-gather.10
